TPU v7x, 32 devices: a whole 2x2x4 slice. The times are simulated.
32 devices in a mesh: side: 2 (over core), dev: 16 (over z, y, x).
Axes of the slice: x: 2, y: 2, z: 4, core: 2. Of those that a mesh axis runs over, the one named last changes fastest.
Arguments:
- out_gates: bfloat16 [512, 2048], P('dev'), may hold values from -6 to 6
- queries: bfloat16 [512, 2048], P('dev'), may hold values from -6 to 6
- keys_new: bfloat16 [512, 256], P('dev'), may hold values from -6 to 6
- values_new: bfloat16 [512, 256], P('dev'), may hold values from -6 to 6
- lengths: int32 [512], P('dev'), may hold values from 1 to 128, as said below
- page_table: int32 [512, 8], P('dev'), may hold values from 0 to 143, as said below
- cache_pool: bfloat16 [2304, 16, 512], P('dev'), may hold values from -1 to 1
- query_gain: float32 [256], replicated, may hold values from 0.25 to 1.75
- key_gain: float32 [256], replicated, may hold values from 0.25 to 1.75
- out_weight: bfloat16 [2048, 2048], replicated, may hold values from -0.125 to 0.125
- residual: bfloat16 [512, 2048], P('dev'), may hold values from -0.625 to 0.625
- post_gain: float32 [2048], replicated, may hold values from 0.25 to 1.75
- experts: int32 [512, 10], P('dev'), may hold values from 0 to 63, all different within a row; in each aligned block of 32 rows (0 to 31, 32 to 63, ...) at most 8 rows name the same one
- route_weights: float32 [512, 10], P('dev'), may hold values from 0.05 to 1
- gate_weight: bfloat16 [64, 2048, 256], P('dev'), may hold values from -0.125 to 0.125
- up_weight: bfloat16 [64, 2048, 256], P('dev'), may hold values from -0.125 to 0.125
- down_weight: bfloat16 [64, 256, 2048], P('dev'), may hold values from -0.375 to 0.375
- shared_gate: bfloat16 [2048, 256], replicated, may hold values from -0.125 to 0.125
- shared_up: bfloat16 [2048, 256], replicated, may hold values from -0.125 to 0.125
- shared_down: bfloat16 [256, 2048], replicated, may hold values from -0.375 to 0.375
- shared_mix: bfloat16 [2048], replicated, may hold values from -0.125 to 0.125
Outputs:
- layer_out: bfloat16 [512, 2048], P('dev', 'side')
Inputs may be any that keep to these rules, and one draw needn't show every extreme that they name: Each row names 10 different experts; the rows of one device (aligned blocks of 32 rows) name one expert at most 8 times. A row's cache fills its first ceil(lengths / 16) page-table entries; in every device some row holds 128 tokens. `page_table`: indices are local to the row's device. The used entries of one device's rows name each of its 144 pages exactly once; unused entries name arbitrary pages.
All inputs are finite; a program needn't handle non-finite values.
Results may differ from a plain program's by a relative error of at most 0.024.
Values may be sent and summed in bfloat16 or wider, within the bound.
A program may use at most 128 MiB of HBM per device.

v0:
```python
import jax
import jax.numpy as jnp
from jax import lax
from jax.sharding import PartitionSpec as P

eps = 1e-06


def from_behind(value, axis, steps):
    count = lax.axis_size(axis)
    first, last = (max(0, -steps), min(count, count - steps))
    return lax.ppermute(value, axis, [(source, source + steps) for source in range(first, last)])


def rms_scale(values, gain):
    wide = values.astype(jnp.float32)
    return wide * lax.rsqrt(jnp.mean(wide * wide, axis=-1, keepdims=True) + eps) * gain


def attend(
    gates_in, queries_in, keys_in, values_in, lengths_in, table_in, cache_pool, query_gain, key_gain
):
    rows = queries_in.shape[0]
    head_dim = keys_in.shape[1]
    heads = queries_in.shape[1] // head_dim
    scale = head_dim ** (-0.5)
    query_normed = rms_scale(queries_in.reshape(rows, heads, head_dim), query_gain).astype(
        jnp.bfloat16
    )
    key_normed = rms_scale(keys_in, key_gain).astype(jnp.bfloat16)
    pages = cache_pool[table_in]
    context = pages.shape[1] * pages.shape[2]
    pages = pages.reshape(rows, context, 2 * head_dim)
    cached_keys = pages[:, :, :head_dim]
    cached_values = pages[:, :, head_dim:]
    scores = (
        jnp.einsum("rhd,rtd->rht", query_normed, cached_keys, preferred_element_type=jnp.float32)
        * scale
    )
    own = (
        jnp.einsum("rhd,rd->rh", query_normed, key_normed, preferred_element_type=jnp.float32)
        * scale
    )
    valid = jnp.arange(context, dtype=jnp.int32)[None, None, :] < lengths_in[:, None, None]
    weights = jnp.where(valid, jnp.exp(scores), 0.0)
    own_weight = jnp.exp(own)
    total = jnp.sum(weights, axis=2) + own_weight
    probs = (weights / total[:, :, None]).astype(jnp.bfloat16)
    own_prob = (own_weight / total).astype(jnp.bfloat16)
    mixed = jnp.einsum("rht,rtd->rhd", probs, cached_values, preferred_element_type=jnp.float32)
    mixed = (
        mixed + own_prob.astype(jnp.float32)[:, :, None] * values_in.astype(jnp.float32)[:, None, :]
    )
    gated = mixed * jax.nn.sigmoid(gates_in.reshape(rows, heads, head_dim).astype(jnp.float32))
    return gated.reshape(rows, heads * head_dim).astype(jnp.bfloat16)


def slot_index(chosen, experts_all, local_experts, capacity):
    flat = chosen.reshape(-1)
    onehot = (flat[:, None] == jnp.arange(experts_all, dtype=jnp.int32)[None, :]).astype(jnp.int32)
    rank = jnp.sum((jnp.cumsum(onehot, axis=0) - 1) * onehot, axis=1)
    owner = flat // local_experts
    return owner * (capacity * local_experts) + rank * local_experts + flat % local_experts


def pack_rows(normed, slots, n_dev, capacity, local_experts):
    topk = slots.shape[0] // normed.shape[0]
    copies = jnp.repeat(normed, topk, axis=0)
    filled = (
        jnp.zeros((n_dev * capacity * local_experts, normed.shape[1]), jnp.bfloat16)
        .at[slots]
        .set(copies)
    )
    return filled.reshape(n_dev, capacity, local_experts, normed.shape[1])


def serve_rows(received, gate_weight, up_weight, down_weight):
    gate_val = jnp.einsum(
        "scud,udf->scuf", received, gate_weight, preferred_element_type=jnp.float32
    )
    up_val = jnp.einsum("scud,udf->scuf", received, up_weight, preferred_element_type=jnp.float32)
    inner = (jax.nn.silu(gate_val) * up_val).astype(jnp.bfloat16)
    return jnp.einsum(
        "scuf,ufd->scud", inner, down_weight, preferred_element_type=jnp.float32
    ).astype(jnp.bfloat16)


def shared_branch(normed, shared_gate, shared_up, shared_down, shared_mix):
    gate_val = jnp.dot(normed, shared_gate, preferred_element_type=jnp.float32)
    up_val = jnp.dot(normed, shared_up, preferred_element_type=jnp.float32)
    inner = (jax.nn.silu(gate_val) * up_val).astype(jnp.bfloat16)
    result = jnp.dot(inner, shared_down, preferred_element_type=jnp.float32)
    weight = jax.nn.sigmoid(jnp.dot(normed, shared_mix, preferred_element_type=jnp.float32))
    return result * weight[:, None]


def combine(hidden, returned, slots, weights_in, shared_out):
    rows, topk = weights_in.shape
    picked = returned[slots].reshape(rows, topk, returned.shape[1])
    share = weights_in / jnp.sum(weights_in, axis=1, keepdims=True)
    routed = jnp.einsum("rk,rkd->rd", share, picked.astype(jnp.float32))
    return (hidden.astype(jnp.float32) + routed + shared_out).astype(jnp.bfloat16)


def on_device(
    out_gates,
    queries,
    keys_new,
    values_new,
    lengths,
    page_table,
    cache_pool,
    query_gain,
    key_gain,
    out_weight,
    residual,
    post_gain,
    experts,
    route_weights,
    gate_weight,
    up_weight,
    down_weight,
    shared_gate,
    shared_up,
    shared_down,
    shared_mix,
):
    n_dev = lax.axis_size("dev")
    local_experts = gate_weight.shape[0]
    experts_all = local_experts * n_dev
    rows_dev, topk = experts.shape
    capacity = max(2, (3 * rows_dev * topk + 2 * experts_all - 1) // (2 * experts_all))
    width = residual.shape[1]
    side = lax.axis_index("side")
    row_args = (
        out_gates,
        queries,
        keys_new,
        values_new,
        lengths,
        page_table,
        residual,
        experts,
        route_weights,
    )

    def front(picked_rows):
        (
            gates_in,
            queries_in,
            keys_in,
            values_in,
            lengths_in,
            table_in,
            residual_in,
            chosen,
            weights_unused,
        ) = picked_rows
        attended = attend(
            gates_in,
            queries_in,
            keys_in,
            values_in,
            lengths_in,
            table_in,
            cache_pool,
            query_gain,
            key_gain,
        )
        projected = jnp.dot(attended, out_weight, preferred_element_type=jnp.float32)
        hidden = (residual_in.astype(jnp.float32) + projected).astype(jnp.bfloat16)
        normed = rms_scale(hidden, post_gain).astype(jnp.bfloat16)
        slots = slot_index(chosen, experts_all, local_experts, capacity)
        return (hidden, normed, slots, pack_rows(normed, slots, n_dev, capacity, local_experts))

    def home_front(unused):
        return front(row_args)

    def away_front(unused):
        return (
            jnp.zeros((rows_dev, width), jnp.bfloat16),
            jnp.zeros((rows_dev, width), jnp.bfloat16),
            jnp.zeros((rows_dev * topk,), jnp.int32),
            jnp.zeros((n_dev, capacity, local_experts, width), jnp.bfloat16),
        )

    hidden, normed, slots, packed = lax.cond(side == 0, home_front, away_front, None)
    moved = lax.all_to_all(packed, "dev", split_axis=0, concat_axis=0, tiled=True)
    received = from_behind(moved, "side", 1)

    def expert_work(unused):
        return (
            serve_rows(received, gate_weight, up_weight, down_weight),
            jnp.zeros((rows_dev, width), jnp.float32),
        )

    def home_work(unused):
        return (
            jnp.zeros_like(received),
            shared_branch(normed, shared_gate, shared_up, shared_down, shared_mix),
        )

    served, shared_out = lax.cond(side == 1, expert_work, home_work, None)
    crossed = from_behind(served, "side", -1)
    returned = lax.all_to_all(crossed, "dev", split_axis=0, concat_axis=0, tiled=True)
    joined = combine(hidden, returned.reshape(-1, width), slots, route_weights, shared_out)
    halves_out = lax.all_to_all(joined, "side", split_axis=1, concat_axis=0, tiled=True)
    return halves_out[:rows_dev]


def solution(mesh):
    placed = (
        P("dev", None),
        P("dev", None),
        P("dev", None),
        P("dev", None),
        P("dev"),
        P("dev", None),
        P("dev", None, None),
        P(),
        P(),
        P(),
        P("dev", None),
        P(),
        P("dev", None),
        P("dev", None),
        P("dev", None, None),
        P("dev", None, None),
        P("dev", None, None),
        P(),
        P(),
        P(),
        P(),
    )
    return jax.shard_map(
        on_device, mesh=mesh, in_specs=placed, out_specs=P("dev", "side"), check_vma=False
    )
```

profile of v0, /device:TPU:15, one launch (start us, length us, event | category | flops | bytes accessed | tf_op | source)
XLA Modules:
  0.0 149.8 jit_solution(12892452729154198443)
XLA Ops:
  0.0 1.8 %conditional.2 = (bf16[32,2048]{1,0:T(8,128)(2,1)S(1)}, s32[320]{0:T(512)S(1)}, bf16[16,8,4,2048]{3,2,1,0:T(4,128)(2,1)S(1)}, f32[32,2048]{1,0:T(8,128)}) conditional(s32[]{:T(128)} %convert_element_type.77, () %tuple.23, (bf16[32,2048]{1,0:T(8,128)(2,1)}, s32[32]{0:T(128)}, bf16[32,2048]{1,0:T(8,128)(2,1)}, f32[256]{0:T(256)}, s32[32,8]{0,1:T(8,128)}, ...), branch_computations={%region_0.0_spmd, %region_1.10_spmd} | conditional | flops 307284224 | bytes 39415288 | solution.py:187
  0.0 1.0 broadcast.231
  1.0 0.7 broadcast.232
  1.8 1.4 copy.65
  3.3 31.4 %all_to_all.26 = bf16[16,8,4,2048]{3,1,2,0:T(8,128)(2,1)S(1)} all-to-all(bf16[16,8,4,2048]{3,1,2,0:T(8,128)(2,1)S(1)} %copy.65), channel_id=1, replica_groups=mesh['side'=2,'dev'=16] {'dev'}, dimensions={0} | all-to-all | bytes 4194304 | tf_op jit(solution)/shard_map/all_to_all | solution.py:188
  34.7 1.3 collective-permute-start
  36.0 31.9 %collective-permute-done = bf16[16,8,4,2048]{3,1,2,0:T(8,128)(2,1)} collective-permute-done((bf16[16,8,4,2048]{3,1,2,0:T(8,128)(2,1)S(1)}, bf16[16,8,4,2048]{3,1,2,0:T(8,128)(2,1)}, u32[]{:S(2)}, u32[]{:S(2)}) %collective-permute-start) | collective-permute-done | bytes 2097184 | tf_op jit(solution)/shard_map/ppermute | solution.py:12
  67.8 10.3 %conditional.3 = (bf16[16,8,4,2048]{3,2,1,0:T(4,128)(2,1)S(1)}, f32[32,2048]{1,0:T(8,128)S(1)}) conditional(s32[]{:T(128)} %convert_element_type.78, (bf16[32,2048]{1,0:T(8,128)(2,1)S(1)}, bf16[2048,256]{1,0:T(8,128)(2,1)S(1)}, bf16[2048,256]{1,0:T(8,128)(2,1)}, bf16[256,2048]{1,0:T(8,128)(2,1)}, bf16[2048]{0:T(1024)(128)(2,1)S(1)}) %tuple.44, ...), branch_computations={%region_11.12_spmd, %region_12.13_spmd} | conditional | flops 1612447744 | bytes 58458188 | solution.py:203
  67.9 4.4 %fusion.26 = f32[16,8,4,256]{3,0,1,2:T(8,128)S(1)} fusion(bf16[16,8,4,2048]{3,1,2,0:T(8,128)(2,1)} %get-tuple-element.172, bf16[4,2048,256]{2,1,0:T(8,128)(2,1)} %get-tuple-element.121), kind=kOutput, calls=%fused_computation.28 | convolution fusion | flops 536870912 | bytes 6815744 | tf_op jit(solution)/shard_map/cond/branch_1_fun/scud,udf->scuf/dot_general | solution.py:78
  72.3 3.3 %fusion.41 = bf16[16,8,4,256]{3,0,1,2:T(8,128)(2,1)S(1)} fusion(bf16[16,8,4,2048]{3,1,2,0:T(8,128)(2,1)} %get-tuple-element.172, bf16[4,2048,256]{2,1,0:T(8,128)(2,1)S(1)} %copy-done.19, f32[16,8,4,256]{3,0,1,2:T(8,128)S(1)} %fusion.26), kind=kOutput, calls=%fused_computation.31 | convolution fusion | flops 537657344 | bytes 7077888 | tf_op jit(solution)/shard_map/cond/branch_1_fun/scud,udf->scuf/dot_general | solution.py:81
  75.6 0.7 fusion.21
  76.3 1.8 %copy.60 = bf16[16,8,4,2048]{3,2,1,0:T(4,128)(2,1)S(1)} copy(bf16[16,8,4,2048]{3,1,0,2:T(8,128)(2,1)S(1)} %fusion.21) | data formatting | bytes 4194304 | tf_op jit(solution)/shard_map
  78.2 2.7 %collective-permute-start.1 = (bf16[16,8,4,2048]{3,2,1,0:T(4,128)(2,1)S(1)}, bf16[16,8,4,2048]{3,2,1,0:T(4,128)(2,1)}, u32[]{:S(2)}, u32[]{:S(2)}) collective-permute-start(bf16[16,8,4,2048]{3,2,1,0:T(4,128)(2,1)S(1)} %get-tuple-element.81), channel_id=1, source_target_pairs={{16,0},{17,1},{18,2},{19,3},{20,4},{21,5},{22,6},{23,7},{24,8},{25... | collective-permute-start | bytes 6291464 | tf_op jit(solution)/shard_map/ppermute | solution.py:12
  80.9 2.6 %collective-permute-done.1 = bf16[16,8,4,2048]{3,2,1,0:T(4,128)(2,1)} collective-permute-done((bf16[16,8,4,2048]{3,2,1,0:T(4,128)(2,1)S(1)}, bf16[16,8,4,2048]{3,2,1,0:T(4,128)(2,1)}, u32[]{:S(2)}, u32[]{:S(2)}) %collective-permute-start.1) | collective-permute-done | bytes 2097184 | tf_op jit(solution)/shard_map/ppermute | solution.py:12
  83.5 6.1 %all-to-all-start.1 = ((bf16[16,8,4,2048]{3,2,1,0:T(4,128)(2,1)}), bf16[16,8,4,2048]{3,2,1,0:T(4,128)(2,1)}, u32[]{:S(2)}, u32[]{:S(2)}) async-start(bf16[16,8,4,2048]{3,2,1,0:T(4,128)(2,1)} %collective-permute-done.1), calls=%async_computation.1 | async-start | bytes 4194304 | tf_op jit(solution)/shard_map/all_to_all | solution.py:205
  89.7 0.1 copy.73
  89.8 48.1 %all-to-all-done.1 = bf16[16,8,4,2048]{3,2,1,0:T(4,128)(2,1)} async-done(((bf16[16,8,4,2048]{3,2,1,0:T(4,128)(2,1)}), bf16[16,8,4,2048]{3,2,1,0:T(4,128)(2,1)}, u32[]{:S(2)}, u32[]{:S(2)}) %all-to-all-start.1) | async-done | bytes 2097184 | tf_op jit(solution)/shard_map/all_to_all | solution.py:205
  137.9 2.5 %reshape.223 = bf16[512,2048]{1,0:T(8,128)(2,1)S(1)} reshape(bf16[16,8,4,2048]{3,2,1,0:T(4,128)(2,1)} %all-to-all-done.1) | data formatting | bytes 4194304 | tf_op jit(solution)/shard_map/reshape | solution.py:206
  140.4 2.4 %gather_fusion.1 = bf16[320,2048]{1,0:T(8,128)(2,1)S(1)} fusion(bf16[512,2048]{1,0:T(8,128)(2,1)S(1)} %reshape.223, s32[1024]{0:T(1024)S(1)} %pad_clamp_fusion.1), kind=kCustom, calls=%fused_computation.1 | custom fusion | bytes 2622720 | tf_op jit(solution)/shard_map/gather | solution.py:99
  142.8 0.5 reshape.224
  143.3 0.4 fusion.95
  143.8 0.5 copy-done.2
  144.5 4.7 %all_to_all.27 = bf16[32,2,1024]{2,0,1:T(8,128)(2,1)S(1)} all-to-all(bf16[32,2,1024]{2,0,1:T(8,128)(2,1)S(1)} %bitcast.106), channel_id=1, replica_groups=mesh['side'=2,'dev'=16] {'side'}, dimensions={1} | all-to-all | bytes 262144 | tf_op jit(solution)/shard_map/all_to_all | solution.py:207
  149.2 0.6 slice_bitcast_fusion
  (24 shorter events, 0.3 us)
Async XLA Ops:
  3.2 64.6 %copy-start.5 = (bf16[2048,256]{1,0:T(8,128)(2,1)S(1)}, bf16[2048,256]{1,0:T(8,128)(2,1)}, u32[]{:S(2)}) copy-start(bf16[2048,256]{1,0:T(8,128)(2,1)} %param.42) | copy-start | bytes 3145732
  3.3 64.6 %copy-start.15 = (bf16[2048]{0:T(1024)(128)(2,1)S(1)}, bf16[2048]{0:T(1024)(128)(2,1)}, u32[]{:S(2)}) copy-start(bf16[2048]{0:T(1024)(128)(2,1)} %param.45) | copy-start | bytes 12292
  34.7 33.2 %collective-permute-start = (bf16[16,8,4,2048]{3,1,2,0:T(8,128)(2,1)S(1)}, bf16[16,8,4,2048]{3,1,2,0:T(8,128)(2,1)}, u32[]{:S(2)}, u32[]{:S(2)}) collective-permute-start(bf16[16,8,4,2048]{3,1,2,0:T(8,128)(2,1)S(1)} %all_to_all.26), channel_id=1, source_target_pairs={{0,16},{1,17},{2,18},{3,19},{4,20},{5,21},{6,22},{7,23},{8,24},{9,... | collective-permute-start | bytes 6291464 | tf_op jit(solution)/shard_map/ppermute | solution.py:12
  67.8 4.4 %copy-start.19 = (bf16[4,2048,256]{2,1,0:T(8,128)(2,1)S(1)}, bf16[4,2048,256]{2,1,0:T(8,128)(2,1)}, u32[]{:S(2)}) copy-start(bf16[4,2048,256]{2,1,0:T(8,128)(2,1)} %get-tuple-element.122) | copy-start | bytes 12582916 | tf_op jit(solution)/shard_map/cond
  72.3 3.3 %copy-start = (bf16[4,256,2048]{2,1,0:T(8,128)(2,1)S(1)}, bf16[4,256,2048]{2,1,0:T(8,128)(2,1)}, u32[]{:S(2)}) copy-start(bf16[4,256,2048]{2,1,0:T(8,128)(2,1)} %get-tuple-element.123) | copy-start | bytes 12582916 | tf_op jit(solution)/shard_map/cond
  78.2 5.4 %copy-start.6 = (f32[32,2048]{1,0:T(8,128)}, f32[32,2048]{1,0:T(8,128)S(1)}, u32[]{:S(2)}) copy-start(f32[32,2048]{1,0:T(8,128)S(1)} %get-tuple-element.83) | copy-start | bytes 786436
  78.2 11.5 %copy-start.11 = (f32[32,10]{0,1:T(8,128)S(1)}, f32[32,10]{0,1:T(8,128)}, u32[]{:S(2)}) copy-start(f32[32,10]{0,1:T(8,128)} %param.38) | copy-start | bytes 3844
  78.2 5.3 %collective-permute-start.1 = (bf16[16,8,4,2048]{3,2,1,0:T(4,128)(2,1)S(1)}, bf16[16,8,4,2048]{3,2,1,0:T(4,128)(2,1)}, u32[]{:S(2)}, u32[]{:S(2)}) collective-permute-start(bf16[16,8,4,2048]{3,2,1,0:T(4,128)(2,1)S(1)} %get-tuple-element.81), channel_id=1, source_target_pairs={{16,0},{17,1},{18,2},{19,3},{20,4},{21,5},{22,6},{23,7},{24,8},{25... | collective-permute-start | bytes 6291464 | tf_op jit(solution)/shard_map/ppermute | solution.py:12
  83.5 54.3 %all-to-all-start.1 = ((bf16[16,8,4,2048]{3,2,1,0:T(4,128)(2,1)}), bf16[16,8,4,2048]{3,2,1,0:T(4,128)(2,1)}, u32[]{:S(2)}, u32[]{:S(2)}) async-start(bf16[16,8,4,2048]{3,2,1,0:T(4,128)(2,1)} %collective-permute-done.1), calls=%async_computation.1 | async-start | bytes 4194304 | tf_op jit(solution)/shard_map/all_to_all | solution.py:205
  143.3 1.0 copy-start.2
  143.3 1.0 copy-start.7
where the time goes:
time: 150 us
  waiting for transfers between devices  82.5 us (55%)
  blocking collectives  36.1 us (24%)
  local copies, waits for them, and re-layouts  11.8 us (8%)
  starting transfers between devices  10.1 us (7%)
  matrix products  8.89 us (6%)
    all_to_all x1, waiting for transfers between devices, on_device(): lax.all_to_all(crossed, 'dev', split_axis=0, concat_axis=0, tiled=True)  48.1 us
    ppermute x2, waiting for transfers between devices, from_behind(): lax.ppermute(value, axis, [(source, source + steps) for source in range(f...  34.5 us
    all_to_all x1, blocking collectives, on_device(): lax.all_to_all(packed, 'dev', split_axis=0, concat_axis=0, tiled=True)  31.4 us
    all_to_all x1, starting transfers between devices, on_device(): lax.all_to_all(crossed, 'dev', split_axis=0, concat_axis=0, tiled=True)  6.12 us
    all_to_all x1, blocking collectives, on_device(): lax.all_to_all(joined, 'side', split_axis=1, concat_axis=0, tiled=True)  4.69 us
    dot_general x1, matrix products, serve_rows(): jnp.einsum('scud,udf->scuf', received, gate_weight, preferred_element_typ...  4.44 us
    ppermute x2, starting transfers between devices, from_behind(): lax.ppermute(value, axis, [(source, source + steps) for source in range(f...  4.01 us
    another operation x6, local copies, waits for them, and re-layouts  3.58 us
  transfers between devices with their start and end apart: 3, of which 3 were waited for; matrix products, arithmetic and copies ran while one was open for 0% of the time, Pallas kernels for 0%

commit v1 on v0

v1 whole, which is shorter than its diff:
```python
import functools

import jax
import jax.numpy as jnp
from jax import lax
from jax.experimental import pallas as pl
from jax.experimental.pallas import tpu as pltpu
from jax.sharding import PartitionSpec as P

eps = 1e-06
MESH = pl.DeviceIdType.MESH
F32 = jnp.float32
BF16 = jnp.bfloat16


def rms_scale(wide, gain):
    return wide * lax.rsqrt(jnp.mean(wide * wide, axis=-1, keepdims=True) + eps) * gain


def sigmoid(value):
    return 1.0 / (1.0 + jnp.exp(-value))


def dot(left, right):
    return jnp.dot(left, right, preferred_element_type=F32)


OUT_CHUNKS = 4


def kernel(
    planes,
    gates_h,
    queries_h,
    keys_h,
    values_h,
    lengths_h,
    table_h,
    pool_h,
    query_gain_h,
    key_gain_h,
    out_weight_h,
    residual_h,
    post_gain_h,
    experts_h,
    route_h,
    gate_weight_h,
    up_weight_h,
    down_weight_h,
    shared_gate_h,
    shared_up_h,
    shared_down_h,
    shared_mix_h,
    out_ref,
    gates,
    queries,
    keys,
    values,
    lengths,
    table,
    pool,
    query_gain,
    key_gain,
    out_weight,
    residual,
    post_gain,
    experts,
    route,
    gate_weight,
    up_weight,
    down_weight,
    shared_gate,
    shared_up,
    shared_down,
    shared_mix,
    gathered,
    select,
    partial,
    diag_in,
    x_in,
    y_in,
    plane_sum,
    z_in,
    base,
    base_out,
    base_in,
    load_sem,
    z_send,
    z_recv,
    x_send,
    x_recv,
    y_send,
    y_recv,
    da_send,
    da_recv,
    db_send,
    db_recv,
    ra_send,
    ra_recv,
    rb_send,
    rb_recv,
    rx_send,
    rx_recv,
    ry_send,
    ry_recv,
    rz_send,
    rz_recv,
    side_sem,
):
    side = lax.axis_index("side")
    dev = lax.axis_index("dev")
    other = 1 - side
    column = lax.rem(dev, 4)
    zi = dev // 4
    x_bit = lax.rem(dev, 2)
    y_bit = lax.rem(dev // 2, 2)
    x_col = column + 1 - 2 * x_bit
    y_col = column + 2 - 4 * y_bit
    d_col = 3 - column
    x_dev = zi * 4 + x_col
    y_dev = zi * 4 + y_col

    rows = queries.shape[0]
    width = residual.shape[1]
    half = width // 2
    wide = gathered.shape[2]
    head_dim = keys.shape[1]
    heads = queries.shape[1] // head_dim
    first = pl.multiple_of(side * rows, rows)

    loads = []

    def load(source, target):
        copy = pltpu.make_async_copy(source, target, load_sem.at[len(loads)])
        copy.start()
        loads.append(copy)
        return copy

    mine = pl.ds(first, rows)
    early = [
        load(queries_h.at[mine], queries),
        load(query_gain_h, query_gain),
        load(lengths_h, lengths),
        load(table_h.at[mine], table),
        load(pool_h, pool),
        load(keys_h.at[mine], keys),
        load(key_gain_h, key_gain),
        load(values_h.at[mine], values),
        load(gates_h.at[mine], gates),
    ]
    step = out_weight.shape[0] // OUT_CHUNKS
    out_loads = [
        load(out_weight_h.at[pl.ds(i * step, step)], out_weight.at[pl.ds(i * step, step)])
        for i in range(OUT_CHUNKS)
    ]
    norm_loads = [
        load(residual_h.at[mine], residual),
        load(post_gain_h, post_gain),
        load(experts_h.at[mine], experts),
        load(route_h.at[mine], route),
    ]
    shared_loads = [
        load(shared_gate_h, shared_gate),
        load(shared_up_h, shared_up),
        load(shared_down_h, shared_down),
        load(shared_mix_h, shared_mix),
    ]
    expert_loads = [
        load(source.at[i], target.at[i])
        for source, target in (
            (gate_weight_h, gate_weight),
            (up_weight_h, up_weight),
            (down_weight_h, down_weight),
        )
        for i in range(gate_weight.shape[0])
    ]

    barrier = pltpu.get_barrier_semaphore()

    def greet(to_side, to_dev):
        pl.semaphore_signal(barrier, inc=1, device_id=(to_side, to_dev), device_id_type=MESH)

    greet(other, dev)
    greet(side, x_dev)
    greet(side, y_dev)
    for k in range(1, planes):
        peer = lax.rem(zi + k, planes) * 4 + column
        greet(side, peer)
        greet(other, peer)

    for copy in early:
        copy.wait()
    tokens = pool.shape[0] * pool.shape[1]
    page = pool.shape[1]
    lane_row = lax.broadcasted_iota(jnp.int32, (rows, lengths.shape[1]), 1)
    sub_row = lax.broadcasted_iota(jnp.int32, (rows, lengths.shape[1]), 0) + first
    length_col = jnp.sum(jnp.where(lane_row == sub_row, lengths[...], 0), axis=1, keepdims=True)
    token = lax.broadcasted_iota(jnp.int32, (rows, tokens), 1)
    token_page = token // page
    token_at = token - token_page * page
    table_val = table[...]
    limit = jnp.zeros((rows, tokens), jnp.int32)
    for j in range(table.shape[1]):
        left = length_col - page * j
        named = jnp.where(left > 0, table_val[:, j : j + 1], -1)
        limit = jnp.where(token_page == named, left, limit)
    valid = jnp.where(limit > token_at, 1.0, 0.0)
    valid = jnp.concatenate([valid] * heads, axis=0)

    def head(value, h):
        return value[:, h * head_dim : (h + 1) * head_dim]

    queries_val = queries[...].astype(F32)
    query_parts = [
        rms_scale(head(queries_val, h), query_gain[...]).astype(BF16) for h in range(heads)
    ]
    key_normed = rms_scale(keys[...].astype(F32), key_gain[...]).astype(BF16).astype(F32)
    own = jnp.concatenate(
        [jnp.sum(q.astype(F32) * key_normed, axis=1, keepdims=True) for q in query_parts], axis=0
    )
    query_all = jnp.concatenate(query_parts, axis=0)
    scale = head_dim ** (-0.5)
    cached_keys = pool[:, :, :head_dim].reshape(tokens, head_dim)
    scores = lax.dot_general(
        query_all, cached_keys, (((1,), (1,)), ((), ())), preferred_element_type=F32
    )
    weights = jnp.where(valid > 0.0, jnp.exp(scores * scale), 0.0)
    own_weight = jnp.exp(own * scale)
    total = jnp.sum(weights, axis=1, keepdims=True) + own_weight
    cached_values = pool[:, :, head_dim:].reshape(tokens, head_dim)
    mixed = dot(weights.astype(BF16), cached_values)
    values_all = jnp.concatenate([values[...].astype(F32)] * heads, axis=0)
    mixed = (mixed + own_weight * values_all) / total
    attended = jnp.concatenate(
        [
            (
                mixed[h * rows : (h + 1) * rows]
                * sigmoid(gates[:, h * head_dim : (h + 1) * head_dim].astype(F32))
            ).astype(BF16)
            for h in range(heads)
        ],
        axis=1,
    )

    projected = jnp.zeros((rows, width), F32)
    for i, copy in enumerate(out_loads):
        copy.wait()
        projected = projected + dot(
            attended[:, i * step : (i + 1) * step], out_weight[i * step : (i + 1) * step, :]
        )
    for copy in norm_loads:
        copy.wait()
    hidden = (residual[...].astype(F32) + projected).astype(BF16).astype(F32)
    normed = rms_scale(hidden, post_gain[...]).astype(BF16)

    route_val = route[...]
    share = route_val / jnp.sum(route_val, axis=1, keepdims=True)
    chosen = experts[...]
    terms = wide - width
    experts_all = terms // 2
    place = lax.broadcasted_iota(jnp.int32, (rows, terms), 1)
    expert_at = lax.rem(place, experts_all)
    spread = jnp.zeros((rows, terms), F32)
    for k in range(experts.shape[1]):
        spread = spread + jnp.where(expert_at == chosen[:, k : k + 1], share[:, k : k + 1], 0.0)
    leading = spread.astype(BF16).astype(F32)
    spread = jnp.where(place < experts_all, leading, spread - leading).astype(BF16)
    gathered[dev] = jnp.concatenate([normed, spread], axis=1)

    pl.semaphore_wait(barrier, 3 + 2 * (planes - 1))

    def remote(source, target, send, recv, to_side, to_dev):
        return pltpu.make_async_remote_copy(
            src_ref=source,
            dst_ref=target,
            send_sem=send,
            recv_sem=recv,
            device_id=(to_side, to_dev),
            device_id_type=MESH,
        )

    def plane(k):
        return lax.rem(zi - k + planes, planes)

    part_a = pl.ds(0, half)
    part_b = pl.ds(half, wide - half)
    out_a = pl.ds(0, half)
    out_b = pl.ds(half, half)

    def send_z(k):
        peer = lax.rem(zi + k, planes) * 4 + column
        return remote(
            gathered.at[dev], gathered.at[dev], z_send.at[k], z_recv.at[k], side, peer
        )

    def send_x(k):
        block = gathered.at[plane(k) * 4 + column]
        return remote(block, block, x_send.at[k], x_recv.at[k], side, x_dev)

    def send_y(k):
        block = gathered.at[plane(k) * 4 + column]
        return remote(block, block, y_send.at[k], y_recv.at[k], side, y_dev)

    def send_da(k):
        block = gathered.at[plane(k) * 4 + x_col, :, part_a]
        return remote(block, block, da_send.at[k], da_recv.at[k], side, y_dev)

    def send_db(k):
        block = gathered.at[plane(k) * 4 + y_col, :, part_b]
        return remote(block, block, db_send.at[k], db_recv.at[k], side, x_dev)

    def send_ra(k):
        return remote(
            partial.at[k, d_col, :, out_a],
            diag_in.at[k, :, out_a],
            ra_send.at[k],
            ra_recv.at[k],
            side,
            x_dev,
        )

    def send_rb(k):
        return remote(
            partial.at[k, d_col, :, out_b],
            diag_in.at[k, :, out_b],
            rb_send.at[k],
            rb_recv.at[k],
            side,
            y_dev,
        )

    def send_rx(k):
        return remote(
            partial.at[k, x_col], x_in.at[k], rx_send.at[k], rx_recv.at[k], side, x_dev
        )

    def send_ry(k):
        return remote(
            partial.at[k, y_col], y_in.at[k], ry_send.at[k], ry_recv.at[k], side, y_dev
        )

    def send_rz(k, to_side):
        columns = pl.ds(pl.multiple_of(to_side * half, half), half)
        return remote(
            plane_sum.at[k, :, columns],
            z_in.at[k, side],
            rz_send.at[k, to_side],
            rz_recv.at[k, side],
            to_side,
            plane(k) * 4 + column,
        )

    def wait_rz(k, from_side):
        columns = pl.ds(pl.multiple_of(side * half, half), half)
        remote(
            plane_sum.at[k, :, columns],
            z_in.at[k, from_side],
            rz_send.at[k, side],
            rz_recv.at[k, from_side],
            side,
            lax.rem(zi + k, planes) * 4 + column,
        ).wait_recv()

    send_x(0).start()
    send_y(0).start()
    for k in range(1, planes):
        send_z(k).start()

    for copy in shared_loads:
        copy.wait()
    gate_val = dot(normed, shared_gate[...])
    up_val = dot(normed, shared_up[...])
    inner = (gate_val * sigmoid(gate_val) * up_val).astype(BF16)
    mix = jnp.sum(normed.astype(F32) * shared_mix[...].astype(F32), axis=1, keepdims=True)
    base[...] = hidden + sigmoid(mix) * dot(inner, shared_down[...])

    local = gate_weight.shape[0]
    hidden_units = gate_weight.shape[2]
    term = lax.broadcasted_iota(jnp.int32, select.shape, 0)
    unit = lax.broadcasted_iota(jnp.int32, select.shape, 1)
    wanted = dev * local + unit // hidden_units
    select[...] = jnp.where(lax.rem(term, experts_all) == wanted, 1.0, 0.0).astype(BF16)

    for k in range(1, planes):
        send_z(k).wait_recv()
        send_x(k).start()
        send_y(k).start()
    for copy in expert_loads:
        copy.wait()

    def forward(k):
        send_x(k).wait_recv()
        send_da(k).start()
        send_y(k).wait_recv()
        send_db(k).start()

    def serve(k):
        send_da(k).wait_recv()
        send_db(k).wait_recv()
        at = pl.ds(pl.multiple_of(plane(k) * 4, 4), 4)
        block = gathered[at].reshape(4 * rows, wide)
        taken = block[:, :width]
        shares = dot(block[:, width:], select[...])
        inners = []
        for i in range(local):
            gate_part = dot(taken, gate_weight[i])
            up_part = dot(taken, up_weight[i])
            weight = shares[:, i * hidden_units : (i + 1) * hidden_units]
            inners.append((gate_part * sigmoid(gate_part) * up_part * weight).astype(BF16))
        inner_all = jnp.concatenate(inners, axis=1)
        down = down_weight[...].reshape(local * hidden_units, width)
        result = dot(inner_all, down).astype(BF16)
        partial[k] = result.reshape(4, rows, width)
        send_ra(k).start()
        send_rb(k).start()

    def reduce_diag(k):
        send_ra(k).wait_recv()
        partial[k, y_col, :, :half] = (
            partial[k, y_col, :, :half].astype(F32) + diag_in[k, :, :half].astype(F32)
        ).astype(BF16)
        send_ry(k).start()
        send_rb(k).wait_recv()
        partial[k, x_col, :, half:] = (
            partial[k, x_col, :, half:].astype(F32) + diag_in[k, :, half:].astype(F32)
        ).astype(BF16)
        send_rx(k).start()

    def reduce_plane(k):
        send_rx(k).wait_recv()
        send_ry(k).wait_recv()
        summed = (
            partial[k, column].astype(F32) + x_in[k].astype(F32) + y_in[k].astype(F32)
        )

        @pl.when(k > 0)
        def _():
            plane_sum[k] = summed.astype(BF16)
            send_rz(k, 0).start()
            send_rz(k, 1).start()

        @pl.when(k == 0)
        def _():
            base[...] = base[...] + summed
            base_out[...] = base[:, pl.ds(pl.multiple_of(other * half, half), half)]
            send_base().start()

    def send_base():
        return remote(base_out, base_in, side_sem.at[0], side_sem.at[1], other, dev)

    forward(0)

    def turn(k, carry):
        @pl.when(k + 1 < planes)
        def _():
            forward(k + 1)

        @pl.when(k < planes)
        def _():
            serve(k)

        @pl.when((k >= 1) & (k <= planes))
        def _():
            reduce_diag(k - 1)

        @pl.when(k >= 2)
        def _():
            reduce_plane(k - 2)

        return carry

    lax.fori_loop(0, planes + 2, turn, 0)

    send_base().wait_recv()
    own_rows = base[:, pl.ds(pl.multiple_of(side * half, half), half)]
    other_rows = base_in[...]
    for k in range(1, planes):
        wait_rz(k, side)
        own_rows = own_rows + z_in[k, side].astype(F32)
        wait_rz(k, other)
        other_rows = other_rows + z_in[k, other].astype(F32)
    out_ref[pl.ds(first, rows), :] = own_rows.astype(BF16)
    out_ref[pl.ds(pl.multiple_of(other * rows, rows), rows), :] = other_rows.astype(BF16)

    def drain(k, carry):
        for send in (send_x, send_y, send_da, send_db, send_ra, send_rb, send_rx, send_ry):
            send(k).wait_send()

        @pl.when(k > 0)
        def _():
            send_z(k).wait_send()
            send_rz(k, 0).wait_send()
            send_rz(k, 1).wait_send()

        return carry

    lax.fori_loop(0, planes, drain, 0)
    send_base().wait_send()


def on_device(
    out_gates,
    queries,
    keys_new,
    values_new,
    lengths,
    page_table,
    cache_pool,
    query_gain,
    key_gain,
    out_weight,
    residual,
    post_gain,
    experts,
    route_weights,
    gate_weight,
    up_weight,
    down_weight,
    shared_gate,
    shared_up,
    shared_down,
    shared_mix,
):
    n_dev = lax.axis_size("dev")
    planes = n_dev // 4
    rows_dev, width = residual.shape
    rows = rows_dev // 2
    half = width // 2
    local, _, hidden_units = gate_weight.shape
    terms = 2 * local * n_dev
    operands = (
        out_gates,
        queries,
        keys_new,
        values_new,
        lengths.reshape(1, -1),
        page_table,
        cache_pool,
        query_gain.reshape(1, -1),
        key_gain.reshape(1, -1),
        out_weight,
        residual,
        post_gain.reshape(1, -1),
        experts,
        route_weights,
        gate_weight,
        up_weight,
        down_weight,
        shared_gate,
        shared_up,
        shared_down,
        shared_mix.reshape(1, -1),
    )
    by_row = (0, 1, 2, 3, 5, 10, 12, 13)
    held = [
        pltpu.VMEM(((rows,) + value.shape[1:]) if i in by_row else value.shape, value.dtype)
        for i, value in enumerate(operands)
    ]
    loads = len(operands) - 4 + OUT_CHUNKS + 3 * local
    per_plane = pltpu.SemaphoreType.DMA((planes,))
    per_side = pltpu.SemaphoreType.DMA((planes, 2))
    flops = 2 * width * (
        width * rows + 3 * hidden_units * rows * (n_dev * local + 1)
    )
    return pl.pallas_call(
        functools.partial(kernel, planes),
        out_shape=jax.ShapeDtypeStruct((rows_dev, half), BF16),
        in_specs=[pl.BlockSpec(memory_space=pl.ANY)] * len(operands),
        out_specs=pl.BlockSpec(memory_space=pltpu.VMEM),
        scratch_shapes=held
        + [
            pltpu.VMEM((n_dev, rows, width + terms), BF16),
            pltpu.VMEM((terms, local * hidden_units), BF16),
            pltpu.VMEM((planes, 4, rows, width), BF16),
            pltpu.VMEM((planes, rows, width), BF16),
            pltpu.VMEM((planes, rows, width), BF16),
            pltpu.VMEM((planes, rows, width), BF16),
            pltpu.VMEM((planes, rows, width), BF16),
            pltpu.VMEM((planes, 2, rows, half), BF16),
            pltpu.VMEM((rows, width), F32),
            pltpu.VMEM((rows, half), F32),
            pltpu.VMEM((rows, half), F32),
            pltpu.SemaphoreType.DMA((loads,)),
        ]
        + [per_plane] * 18
        + [per_side] * 2
        + [pltpu.SemaphoreType.DMA((2,))],
        compiler_params=pltpu.CompilerParams(
            collective_id=0, has_side_effects=True, vmem_limit_bytes=56 * 1024 * 1024
        ),
        cost_estimate=pl.CostEstimate(
            flops=flops, bytes_accessed=27 * 1024 * 1024, transcendentals=1024 * 1024
        ),
    )(*operands)


def solution(mesh):
    placed = (
        P("dev", None),
        P("dev", None),
        P("dev", None),
        P("dev", None),
        P("dev"),
        P("dev", None),
        P("dev", None, None),
        P(),
        P(),
        P(),
        P("dev", None),
        P(),
        P("dev", None),
        P("dev", None),
        P("dev", None, None),
        P("dev", None, None),
        P("dev", None, None),
        P(),
        P(),
        P(),
        P(),
    )
    return jax.shard_map(
        on_device, mesh=mesh, in_specs=placed, out_specs=P("dev", "side"), check_vma=False
    )
```

time: 150 us -> 52.8 us (0.35)
  the two profiles are of different devices: /device:TPU:15 before, /device:TPU:0 now
where the time goes in v1:
time: 52.8 us; the launch traced here: 52.5 us
  Pallas kernels  45.6 us (86%)
  local copies, waits for them, and re-layouts  6.87 us (13%)
    pallas_call x1, Pallas kernels, on_device(): pl.pallas_call(functools.partial(kernel, planes), out_shape=jax.ShapeDtyp...  45.6 us
    unnamed x4, local copies, waits for them, and re-layouts  5.58 us
    reshape x1, local copies, waits for them, and re-layouts, on_device(): shared_mix.reshape(1, -1)  1.29 us

profile of v1, /device:TPU:0, one launch (start us, length us, event | category | flops | bytes accessed | tf_op | source)
XLA Modules:
  0.0 52.5 jit_solution(5414379350819464518)
XLA Ops:
  0.0 1.3 %reshape.19.shared_mix_h = bf16[1,2048]{1,0:T(2,128)(2,1)} reshape(bf16[2048]{0:T(1024)(128)(2,1)} %param.41) | data formatting | bytes 8192 | tf_op jit(solution)/shard_map/reshape | solution.py:552
  1.3 1.4 %copy.22.table_h = s32[32,8]{1,0:T(8,128)} copy(s32[32,8]{0,1:T(8,128)} %param.26) | data formatting | bytes 2048 | tf_op args[5]
  2.7 1.4 %copy.23.experts_h = s32[32,10]{1,0:T(8,128)} copy(s32[32,10]{0,1:T(8,128)} %param.33) | data formatting | bytes 2560 | tf_op args[12]
  4.0 1.4 %copy.24.route_h = f32[32,10]{1,0:T(8,128)} copy(f32[32,10]{0,1:T(8,128)} %param.34) | data formatting | bytes 2560 | tf_op args[13]
  5.4 45.6 %shard_map.199 = bf16[32,1024]{1,0:T(8,128)(2,1)} custom-call(bf16[32,2048]{1,0:T(8,128)(2,1)} %gates_h.1, bf16[32,2048]{1,0:T(8,128)(2,1)} %queries_h.1, bf16[32,256]{1,0:T(8,128)(2,1)} %keys_h.1, bf16[32,256]{1,0:T(8,128)(2,1)} %values_h.1, s32[1,32]{1,0:T(1,128)} %bitcast.7, s32[32,8]{1,0:T(8,128)} %copy.22.table_h, bf16[144,16,512]{2,1,0:T(8,128)(2,1)} %pool_h.1, ...), custom_call_target="tpu_custom_call" | custom-call | flops 3405774848 | bytes 28311552 | tf_op jit(solution)/shard_map/pallas_call | solution.py:565
  51.0 1.5 %copy.26 = bf16[32,1024]{1,0:T(8,128)(2,1)} copy(bf16[32,1024]{1,0:T(8,128)(2,1)} %shard_map.199) | data formatting | bytes 131072

commit v2 on v1

--- a/solution.py
+++ b/solution.py
@@ -23,6 +23,18 @@
 
 def dot(left, right):
     return jnp.dot(left, right, preferred_element_type=F32)
+
+
+def quotient(value, by):
+    if by & (by - 1) == 0:
+        return lax.shift_right_logical(value, jnp.full_like(value, by.bit_length() - 1))
+    return value // by
+
+
+def remainder(value, by):
+    if by & (by - 1) == 0:
+        return value & (by - 1)
+    return lax.rem(value, by)
 
 
 OUT_CHUNKS = 4
@@ -137,28 +149,97 @@
         return copy
 
     mine = pl.ds(first, rows)
-    early = [
+    small_loads = [
         load(queries_h.at[mine], queries),
         load(query_gain_h, query_gain),
-        load(lengths_h, lengths),
-        load(table_h.at[mine], table),
-        load(pool_h, pool),
         load(keys_h.at[mine], keys),
         load(key_gain_h, key_gain),
+        load(lengths_h, lengths),
+        load(table_h, table),
+        load(experts_h, experts),
+        load(route_h, route),
+    ]
+    pool_load = load(pool_h, pool)
+    late_loads = [
         load(values_h.at[mine], values),
         load(gates_h.at[mine], gates),
+        load(residual_h.at[mine], residual),
+        load(post_gain_h, post_gain),
     ]
     step = out_weight.shape[0] // OUT_CHUNKS
     out_loads = [
         load(out_weight_h.at[pl.ds(i * step, step)], out_weight.at[pl.ds(i * step, step)])
         for i in range(OUT_CHUNKS)
     ]
-    norm_loads = [
-        load(residual_h.at[mine], residual),
-        load(post_gain_h, post_gain),
-        load(experts_h.at[mine], experts),
-        load(route_h.at[mine], route),
+
+    barrier = pltpu.get_barrier_semaphore()
+
+    def greet(to_side, to_dev):
+        pl.semaphore_signal(barrier, inc=1, device_id=(to_side, to_dev), device_id_type=MESH)
+
+    greet(other, dev)
+    greet(side, x_dev)
+    greet(side, y_dev)
+    for k in range(1, planes):
+        peer = lax.rem(zi + k, planes) * 4 + column
+        greet(side, peer)
+        greet(other, peer)
+
+    for copy in small_loads:
+        copy.wait()
+
+    lane_row = lax.broadcasted_iota(jnp.int32, (rows, lengths.shape[1]), 1)
+    sub_row = lax.broadcasted_iota(jnp.int32, (rows, lengths.shape[1]), 0) + first
+    picked = lane_row == sub_row
+
+    def as_column(line):
+        return jnp.sum(jnp.where(picked, line, jnp.zeros_like(line)), axis=1, keepdims=True)
+
+    width_terms = wide - width
+    experts_all = width_terms // 2
+    route_val = route[...]
+    share = route_val / jnp.sum(route_val, axis=0, keepdims=True)
+    chosen = experts[...]
+    place = lax.broadcasted_iota(jnp.int32, (rows, width_terms), 1)
+    expert_at = remainder(place, experts_all)
+    spread = jnp.zeros((rows, width_terms), F32)
+    for k in range(experts.shape[0]):
+        spread = spread + jnp.where(
+            expert_at == as_column(chosen[k : k + 1]), as_column(share[k : k + 1]), 0.0
+        )
+    leading = spread.astype(BF16).astype(F32)
+    spread = jnp.where(place < experts_all, leading, spread - leading).astype(BF16)
+
+    tokens = pool.shape[0] * pool.shape[1]
+    page = pool.shape[1]
+    length_col = as_column(lengths[...])
+    token = lax.broadcasted_iota(jnp.int32, (rows, tokens), 1)
+    token_page = quotient(token, page)
+    token_at = remainder(token, page)
+    table_val = table[...]
+    limit = jnp.zeros((rows, tokens), jnp.int32)
+    for j in range(table.shape[0]):
+        left = length_col - page * j
+        named = jnp.where(left > 0, as_column(table_val[j : j + 1]), -1)
+        limit = jnp.where(token_page == named, left, limit)
+    valid = jnp.where(limit > token_at, 1.0, 0.0)
+    valid = jnp.concatenate([valid] * heads, axis=0)
+
+    def head(value, h):
+        return value[:, h * head_dim : (h + 1) * head_dim]
+
+    queries_val = queries[...].astype(F32)
+    query_parts = [
+        rms_scale(head(queries_val, h), query_gain[...]).astype(BF16) for h in range(heads)
     ]
+    key_normed = rms_scale(keys[...].astype(F32), key_gain[...]).astype(BF16).astype(F32)
+    own = jnp.concatenate(
+        [jnp.sum(q.astype(F32) * key_normed, axis=1, keepdims=True) for q in query_parts], axis=0
+    )
+    query_all = jnp.concatenate(query_parts, axis=0)
+    scale = head_dim ** (-0.5)
+    pool_load.wait()
+    cached_keys = pool[:, :, :head_dim].reshape(tokens, head_dim)
     shared_loads = [
         load(shared_gate_h, shared_gate),
         load(shared_up_h, shared_up),
@@ -174,53 +255,6 @@
         )
         for i in range(gate_weight.shape[0])
     ]
-
-    barrier = pltpu.get_barrier_semaphore()
-
-    def greet(to_side, to_dev):
-        pl.semaphore_signal(barrier, inc=1, device_id=(to_side, to_dev), device_id_type=MESH)
-
-    greet(other, dev)
-    greet(side, x_dev)
-    greet(side, y_dev)
-    for k in range(1, planes):
-        peer = lax.rem(zi + k, planes) * 4 + column
-        greet(side, peer)
-        greet(other, peer)
-
-    for copy in early:
-        copy.wait()
-    tokens = pool.shape[0] * pool.shape[1]
-    page = pool.shape[1]
-    lane_row = lax.broadcasted_iota(jnp.int32, (rows, lengths.shape[1]), 1)
-    sub_row = lax.broadcasted_iota(jnp.int32, (rows, lengths.shape[1]), 0) + first
-    length_col = jnp.sum(jnp.where(lane_row == sub_row, lengths[...], 0), axis=1, keepdims=True)
-    token = lax.broadcasted_iota(jnp.int32, (rows, tokens), 1)
-    token_page = token // page
-    token_at = token - token_page * page
-    table_val = table[...]
-    limit = jnp.zeros((rows, tokens), jnp.int32)
-    for j in range(table.shape[1]):
-        left = length_col - page * j
-        named = jnp.where(left > 0, table_val[:, j : j + 1], -1)
-        limit = jnp.where(token_page == named, left, limit)
-    valid = jnp.where(limit > token_at, 1.0, 0.0)
-    valid = jnp.concatenate([valid] * heads, axis=0)
-
-    def head(value, h):
-        return value[:, h * head_dim : (h + 1) * head_dim]
-
-    queries_val = queries[...].astype(F32)
-    query_parts = [
-        rms_scale(head(queries_val, h), query_gain[...]).astype(BF16) for h in range(heads)
-    ]
-    key_normed = rms_scale(keys[...].astype(F32), key_gain[...]).astype(BF16).astype(F32)
-    own = jnp.concatenate(
-        [jnp.sum(q.astype(F32) * key_normed, axis=1, keepdims=True) for q in query_parts], axis=0
-    )
-    query_all = jnp.concatenate(query_parts, axis=0)
-    scale = head_dim ** (-0.5)
-    cached_keys = pool[:, :, :head_dim].reshape(tokens, head_dim)
     scores = lax.dot_general(
         query_all, cached_keys, (((1,), (1,)), ((), ())), preferred_element_type=F32
     )
@@ -229,6 +263,8 @@
     total = jnp.sum(weights, axis=1, keepdims=True) + own_weight
     cached_values = pool[:, :, head_dim:].reshape(tokens, head_dim)
     mixed = dot(weights.astype(BF16), cached_values)
+    for copy in late_loads:
+        copy.wait()
     values_all = jnp.concatenate([values[...].astype(F32)] * heads, axis=0)
     mixed = (mixed + own_weight * values_all) / total
     attended = jnp.concatenate(
@@ -242,29 +278,22 @@
         axis=1,
     )
 
+    local = gate_weight.shape[0]
+    hidden_units = gate_weight.shape[2]
+    term = lax.broadcasted_iota(jnp.int32, (select.shape[0], 1), 0)
+    unit = lax.broadcasted_iota(jnp.int32, (1, select.shape[1]), 1)
+    wanted = dev * local + quotient(unit, hidden_units)
+    select[...] = jnp.where(remainder(term, experts_all) == wanted, 1.0, 0.0).astype(BF16)
+
     projected = jnp.zeros((rows, width), F32)
     for i, copy in enumerate(out_loads):
         copy.wait()
         projected = projected + dot(
             attended[:, i * step : (i + 1) * step], out_weight[i * step : (i + 1) * step, :]
         )
-    for copy in norm_loads:
-        copy.wait()
     hidden = (residual[...].astype(F32) + projected).astype(BF16).astype(F32)
     normed = rms_scale(hidden, post_gain[...]).astype(BF16)
 
-    route_val = route[...]
-    share = route_val / jnp.sum(route_val, axis=1, keepdims=True)
-    chosen = experts[...]
-    terms = wide - width
-    experts_all = terms // 2
-    place = lax.broadcasted_iota(jnp.int32, (rows, terms), 1)
-    expert_at = lax.rem(place, experts_all)
-    spread = jnp.zeros((rows, terms), F32)
-    for k in range(experts.shape[1]):
-        spread = spread + jnp.where(expert_at == chosen[:, k : k + 1], share[:, k : k + 1], 0.0)
-    leading = spread.astype(BF16).astype(F32)
-    spread = jnp.where(place < experts_all, leading, spread - leading).astype(BF16)
     gathered[dev] = jnp.concatenate([normed, spread], axis=1)
 
     pl.semaphore_wait(barrier, 3 + 2 * (planes - 1))
@@ -366,27 +395,10 @@
     for k in range(1, planes):
         send_z(k).start()
 
-    for copy in shared_loads:
-        copy.wait()
-    gate_val = dot(normed, shared_gate[...])
-    up_val = dot(normed, shared_up[...])
-    inner = (gate_val * sigmoid(gate_val) * up_val).astype(BF16)
-    mix = jnp.sum(normed.astype(F32) * shared_mix[...].astype(F32), axis=1, keepdims=True)
-    base[...] = hidden + sigmoid(mix) * dot(inner, shared_down[...])
-
-    local = gate_weight.shape[0]
-    hidden_units = gate_weight.shape[2]
-    term = lax.broadcasted_iota(jnp.int32, select.shape, 0)
-    unit = lax.broadcasted_iota(jnp.int32, select.shape, 1)
-    wanted = dev * local + unit // hidden_units
-    select[...] = jnp.where(lax.rem(term, experts_all) == wanted, 1.0, 0.0).astype(BF16)
-
-    for k in range(1, planes):
+    def relay(k):
         send_z(k).wait_recv()
         send_x(k).start()
         send_y(k).start()
-    for copy in expert_loads:
-        copy.wait()
 
     def forward(k):
         send_x(k).wait_recv()
@@ -449,8 +461,27 @@
         return remote(base_out, base_in, side_sem.at[0], side_sem.at[1], other, dev)
 
     forward(0)
+    if planes > 1:
+        relay(1)
+
+    for copy in shared_loads:
+        copy.wait()
+    gate_val = dot(normed, shared_gate[...])
+    up_val = dot(normed, shared_up[...])
+    inner = (gate_val * sigmoid(gate_val) * up_val).astype(BF16)
+    mix_rows = shared_mix[...].astype(F32)
+    mix_row = jnp.concatenate([mix_rows[i : i + 1] for i in range(mix_rows.shape[0])], axis=1)
+    mix = jnp.sum(normed.astype(F32) * mix_row, axis=1, keepdims=True)
+    base[...] = hidden + sigmoid(mix) * dot(inner, shared_down[...])
+
+    for copy in expert_loads:
+        copy.wait()
 
     def turn(k, carry):
+        @pl.when(k + 2 < planes)
+        def _():
+            relay(k + 2)
+
         @pl.when(k + 1 < planes)
         def _():
             forward(k + 1)
@@ -534,24 +565,24 @@
         keys_new,
         values_new,
         lengths.reshape(1, -1),
-        page_table,
+        page_table.T,
         cache_pool,
         query_gain.reshape(1, -1),
         key_gain.reshape(1, -1),
         out_weight,
         residual,
         post_gain.reshape(1, -1),
-        experts,
-        route_weights,
+        experts.T,
+        route_weights.T,
         gate_weight,
         up_weight,
         down_weight,
         shared_gate,
         shared_up,
         shared_down,
-        shared_mix.reshape(1, -1),
+        shared_mix.reshape(-1, 128),
     )
-    by_row = (0, 1, 2, 3, 5, 10, 12, 13)
+    by_row = (0, 1, 2, 3, 10)
     held = [
         pltpu.VMEM(((rows,) + value.shape[1:]) if i in by_row else value.shape, value.dtype)
         for i, value in enumerate(operands)

time: 52.8 us -> 42.6 us (0.81)
  local copies, waits for them, and re-layouts: 6.87 us -> 1.47 us
  Pallas kernels: 45.6 us -> 41 us
    pallas_call x1, Pallas kernels: 45.6 us -> 41 us  [on_device(): pl.pallas_call(functools.partial(kernel, planes), out_shape=jax.ShapeDtyp...]
    unnamed x4 -> x1, local copies, waits for them, and re-layouts: 5.58 us -> 1.47 us
    reshape x1 -> x0, local copies, waits for them, and re-layouts: 1.29 us -> none  [on_device(): shared_mix.reshape(1, -1)]
where the time goes in v2:
time: 42.6 us; the launch traced here: 42.5 us
  Pallas kernels  41 us (96%)
  local copies, waits for them, and re-layouts  1.47 us (3%)
    pallas_call x1, Pallas kernels, on_device(): pl.pallas_call(functools.partial(kernel, planes), out_shape=jax.ShapeDtyp...  41 us
    unnamed x1, local copies, waits for them, and re-layouts  1.47 us

profile of v2, /device:TPU:0, one launch (start us, length us, event | category | flops | bytes accessed | tf_op | source)
XLA Modules:
  0.0 42.5 jit_solution(6971129161958425030)
XLA Ops:
  0.0 41.0 %shard_map.199 = bf16[32,1024]{1,0:T(8,128)(2,1)} custom-call(bf16[32,2048]{1,0:T(8,128)(2,1)} %gates_h.1, bf16[32,2048]{1,0:T(8,128)(2,1)} %queries_h.1, bf16[32,256]{1,0:T(8,128)(2,1)} %keys_h.1, bf16[32,256]{1,0:T(8,128)(2,1)} %values_h.1, s32[1,32]{1,0:T(1,128)} %bitcast.15, s32[8,32]{1,0:T(8,128)} %bitcast.11, bf16[144,16,512]{2,1,0:T(8,128)(2,1)} %pool_h.1, ...), custom_call_target="tpu_custom_call" | custom-call | flops 3405774848 | bytes 28311552 | tf_op jit(solution)/shard_map/pallas_call | solution.py:596
  41.0 1.5 %copy.23 = bf16[32,1024]{1,0:T(8,128)(2,1)} copy(bf16[32,1024]{1,0:T(8,128)(2,1)} %shard_map.199) | data formatting | bytes 131072

commit v3 on v2

--- a/solution.py
+++ b/solution.py
@@ -240,21 +240,6 @@
     scale = head_dim ** (-0.5)
     pool_load.wait()
     cached_keys = pool[:, :, :head_dim].reshape(tokens, head_dim)
-    shared_loads = [
-        load(shared_gate_h, shared_gate),
-        load(shared_up_h, shared_up),
-        load(shared_down_h, shared_down),
-        load(shared_mix_h, shared_mix),
-    ]
-    expert_loads = [
-        load(source.at[i], target.at[i])
-        for source, target in (
-            (gate_weight_h, gate_weight),
-            (up_weight_h, up_weight),
-            (down_weight_h, down_weight),
-        )
-        for i in range(gate_weight.shape[0])
-    ]
     scores = lax.dot_general(
         query_all, cached_keys, (((1,), (1,)), ((), ())), preferred_element_type=F32
     )
@@ -285,6 +270,21 @@
     wanted = dev * local + quotient(unit, hidden_units)
     select[...] = jnp.where(remainder(term, experts_all) == wanted, 1.0, 0.0).astype(BF16)
 
+    shared_loads = [
+        load(shared_gate_h, shared_gate),
+        load(shared_up_h, shared_up),
+        load(shared_down_h, shared_down),
+        load(shared_mix_h, shared_mix),
+    ]
+    expert_loads = [
+        load(source.at[i], target.at[i])
+        for source, target in (
+            (gate_weight_h, gate_weight),
+            (up_weight_h, up_weight),
+            (down_weight_h, down_weight),
+        )
+        for i in range(gate_weight.shape[0])
+    ]
     projected = jnp.zeros((rows, width), F32)
     for i, copy in enumerate(out_loads):
         copy.wait()
@@ -423,8 +423,16 @@
         down = down_weight[...].reshape(local * hidden_units, width)
         result = dot(inner_all, down).astype(BF16)
         partial[k] = result.reshape(4, rows, width)
-        send_ra(k).start()
-        send_rb(k).start()
+
+        @pl.when(k > 0)
+        def _():
+            send_ra(k).start()
+            send_rb(k).start()
+
+        @pl.when(k == planes - 1)
+        def _():
+            send_ra(0).start()
+            send_rb(0).start()
 
     def reduce_diag(k):
         send_ra(k).wait_recv()
@@ -490,17 +498,17 @@
         def _():
             serve(k)
 
-        @pl.when((k >= 1) & (k <= planes))
-        def _():
-            reduce_diag(k - 1)
-
-        @pl.when(k >= 2)
-        def _():
-            reduce_plane(k - 2)
+        @pl.when((k >= 2) & (k <= planes + 1))
+        def _():
+            reduce_diag(lax.rem(k - 1, planes))
+
+        @pl.when(k >= 3)
+        def _():
+            reduce_plane(lax.rem(k - 2, planes))
 
         return carry
 
-    lax.fori_loop(0, planes + 2, turn, 0)
+    lax.fori_loop(0, planes + 3, turn, 0)
 
     send_base().wait_recv()
     own_rows = base[:, pl.ds(pl.multiple_of(side * half, half), half)]

time: 42.6 us -> 41.9 us (0.984)
  Pallas kernels: 41 us -> 40.3 us
    pallas_call x1, Pallas kernels: 41 us -> 40.3 us  [on_device(): pl.pallas_call(functools.partial(kernel, planes), out_shape=jax.ShapeDtyp...]
where the time goes in v3:
time: 41.9 us; the launch traced here: 41.8 us
  Pallas kernels  40.3 us (96%)
  local copies, waits for them, and re-layouts  1.47 us (4%)
    pallas_call x1, Pallas kernels, on_device(): pl.pallas_call(functools.partial(kernel, planes), out_shape=jax.ShapeDtyp...  40.3 us
    unnamed x1, local copies, waits for them, and re-layouts  1.47 us

profile of v3, /device:TPU:0, one launch (start us, length us, event | category | flops | bytes accessed | tf_op | source)
XLA Modules:
  0.0 41.8 jit_solution(1801119269988457778)
XLA Ops:
  0.0 40.3 %shard_map.199 = bf16[32,1024]{1,0:T(8,128)(2,1)} custom-call(bf16[32,2048]{1,0:T(8,128)(2,1)} %gates_h.1, bf16[32,2048]{1,0:T(8,128)(2,1)} %queries_h.1, bf16[32,256]{1,0:T(8,128)(2,1)} %keys_h.1, bf16[32,256]{1,0:T(8,128)(2,1)} %values_h.1, s32[1,32]{1,0:T(1,128)} %bitcast.15, s32[8,32]{1,0:T(8,128)} %bitcast.11, bf16[144,16,512]{2,1,0:T(8,128)(2,1)} %pool_h.1, ...), custom_call_target="tpu_custom_call" | custom-call | flops 3405774848 | bytes 28311552 | tf_op jit(solution)/shard_map/pallas_call | solution.py:604
  40.3 1.5 %copy.23 = bf16[32,1024]{1,0:T(8,128)(2,1)} copy(bf16[32,1024]{1,0:T(8,128)(2,1)} %shard_map.199) | data formatting | bytes 131072
